TPU v7x, 32 devices: a whole 2x2x4 slice. The times are simulated.
32 devices in a mesh: lat: 4 (over y, x), lon: 8 (over z, core).
Axes of the slice: x: 2, y: 2, z: 4, core: 2. Of those that a mesh axis runs over, the one named last changes fastest.
Arguments:
- tracers: float32 [2, 3, 1024, 1024], P(None, None, 'lat', 'lon'), may hold values from -6 to 6
- east_courant: float32 [3, 1024, 1024], P(None, 'lat', 'lon'), may hold values from -0.45 to 0.45
- north_courant: float32 [3, 1024, 1024], P(None, 'lat', 'lon'), may hold values from -0.45 to 0.45
- east_kappa: float32 [3, 1024, 1024], P(None, 'lat', 'lon'), may hold values from 0.01 to 0.1
- north_kappa: float32 [3, 1024, 1024], P(None, 'lat', 'lon'), may hold values from 0.01 to 0.1
- ocean_mask: int32 [3, 1024, 1024], P(None, 'lat', 'lon'), may hold values 0 or 1
- fold_map: int32 [1024], P('lon'), may hold values from 0 to 1023, as said below
Outputs:
- updated: float32 [2, 3, 1024, 1024], P(None, None, 'lat', 'lon')
Inputs may be any that keep to these rules, and one draw needn't show every extreme that they name: fold_map[i] = (P - 1 - i) mod 1024 for every column i, with one pivot P that is a multiple of 128.
All inputs are finite; a program needn't handle non-finite values. No bound on the sum of `ocean_mask` on one device may be relied on, other than what follows from the above.
Results may differ from a plain program's by a relative error of at most 0.00002.
Values sent between devices are 32-bit elements; how exact they have to be, the bound alone decides.
A program may use at most 64 MiB of HBM per device.

v0:
```python
import jax
import jax.numpy as jnp
from jax import lax
from jax.sharding import PartitionSpec as P

STEPS = 2


def extended(cells, sides, width, closed):
    for axis, dim in sides:
        count = lax.axis_size(axis)
        ends = count if closed else count - 1
        head = lax.slice_in_dim(cells, 0, width, axis=dim)
        tail = lax.slice_in_dim(cells, cells.shape[dim] - width, cells.shape[dim], axis=dim)
        cells = jnp.concatenate(
            [
                lax.ppermute(tail, axis, [(i, (i + 1) % count) for i in range(ends)]),
                cells,
                lax.ppermute(head, axis, [((i + 1) % count, i) for i in range(ends)]),
            ],
            axis=dim,
        )
    return cells


def face_flux(behind, center, forward, beyond, courant, diffusivity, opened):
    centered = 7.0 * (center + forward) - (behind + beyond)
    upwind = 3.0 * (forward - center) - (beyond - behind)
    return opened * (
        courant * centered / 12.0
        - jnp.abs(courant) * upwind / 12.0
        - diffusivity * (forward - center)
    )


def local(tracers, east_courant, north_courant, east_kappa, north_kappa, ocean_mask, fold_map):
    row_count = tracers.shape[2]
    col_count = tracers.shape[3]
    levels = ocean_mask.shape[0]
    ocean = ocean_mask.astype(jnp.float32)
    lat_index = lax.axis_index("lat")
    southern = lat_index == 0
    northern = lat_index == lax.axis_size("lat") - 1
    coefficients = jnp.concatenate(
        [east_courant, north_courant, east_kappa, north_kappa, ocean], axis=0
    )
    padded = extended(coefficients, (("lat", 1), ("lon", 2)), 1, True)

    def member(which):
        return padded[which * levels : (which + 1) * levels]

    inner_rows = slice(1, row_count + 1)
    east_c = member(0)[:, inner_rows, 1 : col_count + 1]
    east_cw = member(0)[:, inner_rows, 0:1]
    east_k = member(2)[:, inner_rows, 1 : col_count + 1]
    east_kw = member(2)[:, inner_rows, 0:1]
    flags = member(4)
    open_east = flags[:, inner_rows, 1 : col_count + 1] * flags[:, inner_rows, 2 : col_count + 2]
    open_west = flags[:, inner_rows, 0:1] * flags[:, inner_rows, 1:2]
    north_c = member(1)[:, 0 : row_count + 1, 1 : col_count + 1]
    north_k = member(3)[:, 0 : row_count + 1, 1 : col_count + 1]
    columns = flags[:, :, 1 : col_count + 1]
    lower = jnp.where(southern, 0.0, columns[:, 0:1])
    upper = jnp.where(northern, columns[:, row_count : row_count + 1], columns[:, row_count + 1 :])
    adjusted = jnp.concatenate([lower, columns[:, 1 : row_count + 1], upper], axis=1)
    open_north = adjusted[:, 0 : row_count + 1] * adjusted[:, 1 : row_count + 2]
    state = tracers * ocean
    for step_index in range(STEPS):
        top = jnp.stack([state[:, :, -1], state[:, :, -2]], axis=2)
        strip = jnp.concatenate([state[:, :, :, :2], state[:, :, :, -2:]], axis=3)
        edges = extended(strip, (("lon", 3),), 2, True)
        western = edges[:, :, :, 0:2]
        eastern = edges[:, :, :, 6:8]
        across = extended(state, (("lat", 2),), 2, False)
        piece = lax.all_gather(top, "lon", axis=3, tiled=True)
        inside = (fold_map >= 0) & (fold_map < piece.shape[3])
        picked = jnp.take(piece, jnp.clip(fold_map, 0, piece.shape[3] - 1), axis=3)
        folded = jnp.where(inside, picked, 0.0)
        across = across.at[:, :, row_count + 2 : row_count + 4].set(
            jnp.where(northern, folded, across[:, :, row_count + 2 : row_count + 4])
        )
        before_one = jnp.concatenate([western[:, :, :, 1:2], state[:, :, :, :-1]], axis=3)
        after_one = jnp.concatenate([state[:, :, :, 1:], eastern[:, :, :, 0:1]], axis=3)
        after_two = jnp.concatenate([state[:, :, :, 2:], eastern], axis=3)
        east_flux = face_flux(before_one, state, after_one, after_two, east_c, east_k, open_east)
        west_face = face_flux(
            western[:, :, :, 0:1],
            western[:, :, :, 1:2],
            state[:, :, :, 0:1],
            state[:, :, :, 1:2],
            east_cw,
            east_kw,
            open_west,
        )
        east_prior = jnp.concatenate([west_face, east_flux[:, :, :, :-1]], axis=3)
        north_flux = face_flux(
            across[:, :, 0 : row_count + 1],
            across[:, :, 1 : row_count + 2],
            across[:, :, 2 : row_count + 3],
            across[:, :, 3 : row_count + 4],
            north_c,
            north_k,
            open_north,
        )
        state = ocean * (
            state - (east_flux - east_prior) - (north_flux[:, :, 1:] - north_flux[:, :, :-1])
        )
    return state


def solution(mesh):
    in_specs = (
        P(None, None, "lat", "lon"),
        P(None, "lat", "lon"),
        P(None, "lat", "lon"),
        P(None, "lat", "lon"),
        P(None, "lat", "lon"),
        P(None, "lat", "lon"),
        P("lon"),
    )
    out_specs = P(None, None, "lat", "lon")
    return jax.shard_map(local, mesh=mesh, in_specs=in_specs, out_specs=out_specs, check_vma=False)
```

profile of v0, /device:TPU:11, one launch (start us, length us, event | category | flops | bytes accessed | tf_op | source)
XLA Modules:
  0.0 112.2 jit_solution(9055460570299874683)
XLA Ops:
  0.0 1.1 convert_element_type.3
  1.1 1.3 %broadcast_multiply_fusion = f32[2,3,256,128]{3,2,1,0:T(8,128)S(1)} fusion(f32[2,3,256,128]{3,2,1,0:T(8,128)} %param.13, f32[3,256,128]{2,1,0:T(8,128)S(1)} %convert_element_type.3), kind=kLoop, calls=%fused_computation.36 | loop fusion | flops 196608 | bytes 1966080 | tf_op jit(solution)/shard_map/mul | solution.py:67
  2.4 2.3 %collective-permute-start.7 = (f32[2,3,2,128]{3,2,1,0:T(2,128)S(1)}, f32[2,3,2,128]{3,2,1,0:T(2,128)S(1)}, u32[]{:S(2)}, u32[]{:S(2)}) collective-permute-start(f32[2,3,2,128]{3,2,1,0:T(2,128)S(1)} %get-tuple-element.54), channel_id=1, source_target_pairs={{8,0},{16,8},{24,16},{9,1},{17,9},{25,17},{10,2},{18,10},{26,18},{... | collective-permute-start | bytes 18440 | tf_op jit(solution)/shard_map/ppermute | solution.py:19
  4.7 4.0 %collective-permute-start.6 = (f32[2,3,2,128]{3,2,1,0:T(2,128)S(1)}, f32[2,3,2,128]{3,2,1,0:T(2,128)S(1)}, u32[]{:S(2)}, u32[]{:S(2)}) collective-permute-start(f32[2,3,2,128]{3,2,1,0:T(2,128)S(1)} %get-tuple-element.53), channel_id=1, source_target_pairs={{0,8},{8,16},{16,24},{1,9},{9,17},{17,25},{2,10},{10,18},{18,26},{... | collective-permute-start | bytes 18440 | tf_op jit(solution)/shard_map/ppermute | solution.py:17
  8.8 0.8 fusion.23
  9.8 1.3 %copy-done = f32[15,256,128]{2,1,0:T(8,128)} copy-done((f32[15,256,128]{2,1,0:T(8,128)}, f32[15,256,128]{2,1,0:T(8,128)S(1)}, u32[]{:S(2)}) %copy-start) | copy-done | bytes 1966104
  11.2 2.3 %collective-permute-start = (f32[15,1,128]{2,0,1:T(8,128)S(1)}, f32[15,1,128]{2,0,1:T(8,128)S(1)}, u32[]{:S(2)}, u32[]{:S(2)}) collective-permute-start(f32[15,1,128]{2,0,1:T(8,128)S(1)} %copy.212), channel_id=1, source_target_pairs={{0,8},{8,16},{16,24},{24,0},{1,9},{9,17},{17,25},{25,1},{2,10},{10... | collective-permute-start | bytes 23048 | tf_op jit(solution)/shard_map/ppermute | solution.py:17
  14.1 3.0 %collective-permute-start.4 = (f32[2,3,256,2]{2,3,1,0:T(2,128)S(1)}, f32[2,3,256,2]{2,3,1,0:T(2,128)S(1)}, u32[]{:S(2)}, u32[]{:S(2)}) collective-permute-start(f32[2,3,256,2]{2,3,1,0:T(2,128)S(1)} %copy.220), channel_id=1, source_target_pairs={{0,1},{1,2},{2,3},{3,4},{4,5},{5,6},{6,7},{7,0},{8,9},{9,10},{10,1... | collective-permute-start | bytes 36872 | tf_op jit(solution)/shard_map/ppermute | solution.py:17
  17.1 1.4 %fusion.19 = (f32[2,3,256,127]{3,2,1,0:T(8,128)}, f32[2,3,256,127]{3,2,1,0:T(8,128)}) fusion(f32[2,3,256,128]{3,2,1,0:T(8,128)S(1)} %broadcast_multiply_fusion), kind=kLoop, calls=%fused_computation.66 | loop fusion | bytes 3121152 | tf_op jit(solution)/shard_map/slice | solution.py:83
  18.5 7.9 %all_gather.6 = f32[2,3,2,1024]{3,2,1,0:T(2,128)S(1)} all-gather(f32[2,3,2,128]{3,2,1,0:T(2,128)S(1)} %pad_maximum_fusion.14), channel_id=1, replica_groups=mesh['lat'=4,'lon'=8] {'lon'}, dimensions={3}, use_global_device_ids=true | all-gather | bytes 55296 | tf_op jit(solution)/shard_map/all_gather | solution.py:75
  26.4 1.1 %slice.348 = f32[2,3,256,126]{3,2,1,0:T(8,128)} slice(f32[2,3,256,128]{3,2,1,0:T(8,128)S(1)} %broadcast_multiply_fusion), slice={[0:2], [0:3], [0:256], [2:128]} | slice | bytes 1548288 | tf_op jit(solution)/shard_map/slice | solution.py:84
  27.6 2.3 %copy.230 = f32[2,3,2,1024]{1,2,3,0:T(2,128)} copy(f32[2,3,2,1024]{3,2,1,0:T(2,128)S(1)} %all_gather.6) | data formatting | bytes 98304 | tf_op jit(solution)/shard_map/all_gather | solution.py:75
  29.9 2.5 %gather_fusion = f32[128,2,3,2]{2,3,1,0:T(2,128)S(1)} fusion(f32[2,3,2,1024]{1,2,3,0:T(2,128)} %copy.230, s32[1024]{0:T(1024)S(1)} %pad_clamp_fusion), kind=kCustom, calls=%fused_computation.clone | custom fusion | bytes 12800 | tf_op jit(solution)/shard_map/jit(_take)/gather | solution.py:77
  33.3 2.1 %fusion.12 = (f32[3,257,128]{2,1,0:T(8,128)S(1)}, f32[3,257,128]{2,1,0:T(8,128)S(1)}, f32[3,257,128]{2,1,0:T(8,128)}) fusion(f32[15,256,128]{2,1,0:T(8,128)} %copy-done, f32[15,1,128]{2,1,0:T(1,128)S(1)} %copy.214), kind=kLoop, calls=%fused_computation.59 | loop fusion | flops 296064 | bytes 3158016 | tf_op jit(solution)/shard_map/abs | solution.py:31
  35.6 2.6 %fusion.13 = (f32[15,258,1]{2,1,0:T(8,128)}, f32[15,258,1]{2,1,0:T(8,128)}) fusion(f32[15,258,128]{2,1,0:T(8,128)S(1)} %pad_maximum_fusion), kind=kLoop, calls=%fused_computation.60 | loop fusion | bytes 61920 | tf_op jit(solution)/shard_map/slice | solution.py:14
  38.1 3.1 %copy.223 = f32[15,258,1]{1,0,2:T(8,128)} copy(f32[15,258,1]{2,1,0:T(8,128)} %get-tuple-element.34) | data formatting | bytes 30960 | tf_op jit(solution)/shard_map/slice | solution.py:14
  41.2 1.6 %collective-permute-start.5 = (f32[15,258,1]{1,0,2:T(8,128)}, f32[15,258,1]{1,0,2:T(8,128)}, u32[]{:S(2)}, u32[]{:S(2)}) collective-permute-start(f32[15,258,1]{1,0,2:T(8,128)} %copy.223), channel_id=1, source_target_pairs={{0,1},{1,2},{2,3},{3,4},{4,5},{5,6},{6,7},{7,0},{8,9},{9,10},{10,1... | collective-permute-start | bytes 46448 | tf_op jit(solution)/shard_map/ppermute | solution.py:17
  42.8 3.1 %copy.216 = f32[15,258,1]{1,0,2:T(8,128)} copy(f32[15,258,1]{2,1,0:T(8,128)} %get-tuple-element.35) | data formatting | bytes 30960 | tf_op jit(solution)/shard_map/slice | solution.py:13
  45.9 1.8 %collective-permute-start.2 = (f32[15,258,1]{1,0,2:T(8,128)}, f32[15,258,1]{1,0,2:T(8,128)}, u32[]{:S(2)}, u32[]{:S(2)}) collective-permute-start(f32[15,258,1]{1,0,2:T(8,128)} %copy.216), channel_id=1, source_target_pairs={{1,0},{2,1},{3,2},{4,3},{5,4},{6,5},{7,6},{0,7},{9,8},{10,9},{11,1... | collective-permute-start | bytes 46448 | tf_op jit(solution)/shard_map/ppermute | solution.py:19
  47.8 2.5 %subtract_multiply_fusion.1 = f32[2,3,257,128]{3,2,1,0:T(8,128)} fusion(f32[2,3,260,128]{3,2,1,0:T(8,128)S(1)} %fusion.11, f32[3,257,128]{2,1,0:T(8,128)} %get-tuple-element.36, f32[3,257,128]{2,1,0:T(8,128)S(1)} %get-tuple-element.30, f32[3,257,128]{2,1,0:T(8,128)S(1)} %get-tuple-element.31, f32[3,257,128]{2,1,0:T(8,128)S(1)} %maximum_multiply_fusion), kind=kLoop, calls=%fused_computation.6 | loop fusion | flops 3158016 | bytes 5526528 | tf_op jit(solution)/shard_map/mul | solution.py:29
  50.3 1.3 %copy.241 = f32[2,3,256,1]{3,2,1,0:T(8,128)} copy(f32[2,3,256,1]{2,3,1,0:T(1,128)S(1)} %get-tuple-element.64) | data formatting | bytes 12288
  51.6 1.2 %copy.225 = f32[2,3,256,1]{3,2,1,0:T(8,128)} copy(f32[2,3,256,1]{2,3,1,0:T(1,128)S(1)} %get-tuple-element.63) | data formatting | bytes 12288 | tf_op jit(solution)/shard_map/slice | solution.py:87
  52.8 0.6 copy-done.34
  53.3 1.3 %copy.219 = f32[2,3,256,1]{3,2,1,0:T(8,128)} copy(f32[2,3,256,1]{2,3,1,0:T(1,128)S(1)} %slice.344) | data formatting | bytes 12288 | tf_op jit(solution)/shard_map/slice | solution.py:83
  54.6 2.0 %copy.222 = f32[2,3,256,2]{3,2,1,0:T(8,128)} copy(f32[2,3,256,2]{2,3,1,0:T(2,128)} %copy-done.34) | data formatting | bytes 24576 | tf_op jit(solution)/shard_map/ppermute | solution.py:19
  56.6 1.5 %fusion.24 = (f32[3,256,1]{1,0,2:T(4,128)S(1)}, f32[3,256]{1,0:T(4,128)}, f32[3,256]{1,0:T(4,128)}, f32[3,256]{1,0:T(4,128)}) fusion(f32[15,258,1]{1,0,2:T(8,128)} %collective-permute-done.5), kind=kLoop, calls=%fused_computation.71 | loop fusion | flops 768 | bytes 21504 | tf_op jit(solution)/shard_map/slice | solution.py:59
  58.2 1.0 copy.224
  59.1 1.2 %fusion.6 = f32[3,256]{1,0:T(4,128)S(1)} fusion(f32[3,256,1]{2,1,0:T(8,128)} %copy.224, f32[3,256,128]{2,1,0:T(8,128)S(1)} %convert_element_type.3), kind=kLoop, calls=%fused_computation.31 | loop fusion | flops 768 | bytes 9216 | tf_op jit(solution)/shard_map/mul | solution.py:59
  60.3 2.7 %copy.217 = f32[15,258,1]{2,1,0:T(8,128)} copy(f32[15,258,1]{1,0,2:T(8,128)} %collective-permute-done.2) | data formatting | bytes 30960 | tf_op jit(solution)/shard_map/ppermute | solution.py:19
  63.0 1.6 %fusion.7 = f32[3,256,128]{2,1,0:T(8,128)S(1)} fusion(f32[15,258,1]{2,1,0:T(8,128)} %copy.217, f32[15,1,128]{2,1,0:T(1,128)} %copy-done.27, f32[15,256,128]{2,1,0:T(8,128)S(1)} %copy-done.2, f32[15,1,128]{2,1,0:T(1,128)} %copy-done.26, s32[3,256,128]{2,1,0:T(8,128)} %param.18), kind=kLoop, calls=%fused_computation.33 | loop fusion | flops 491520 | bytes 2783352 | tf_op jit(solution)/shard_map/mul | solution.py:58
  64.7 0.7 subtract_multiply_fusion.4
  65.5 0.6 copy-done.4
  66.9 0.8 subtract_multiply_fusion.5
  68.7 1.4 %fusion.15 = (f32[2,3,256,127]{3,2,1,0:T(8,128)}, f32[2,3,256,127]{3,2,1,0:T(8,128)}) fusion(f32[2,3,256,128]{3,2,1,0:T(8,128)S(1)} %fusion.3), kind=kLoop, calls=%fused_computation.62 | loop fusion | bytes 3121152 | tf_op jit(solution)/shard_map/slice | solution.py:83
  70.1 1.2 %slice.377 = f32[2,3,256,126]{3,2,1,0:T(8,128)} slice(f32[2,3,256,128]{3,2,1,0:T(8,128)S(1)} %fusion.3), slice={[0:2], [0:3], [0:256], [2:128]} | slice | bytes 1548288 | tf_op jit(solution)/shard_map/slice | solution.py:84
  71.8 1.8 %collective-permute-start.8 = (f32[2,3,256,2]{2,3,1,0:T(2,128)S(1)}, f32[2,3,256,2]{2,3,1,0:T(2,128)S(1)}, u32[]{:S(2)}, u32[]{:S(2)}) collective-permute-start(f32[2,3,256,2]{2,3,1,0:T(2,128)S(1)} %copy.232), channel_id=1, source_target_pairs={{1,0},{2,1},{3,2},{4,3},{5,4},{6,5},{7,6},{0,7},{9,8},{10,9},{11,1... | collective-permute-start | bytes 36872 | tf_op jit(solution)/shard_map/ppermute | solution.py:19
  73.6 1.9 %collective-permute-start.10 = (f32[2,3,2,128]{3,2,1,0:T(2,128)S(1)}, f32[2,3,2,128]{3,2,1,0:T(2,128)S(1)}, u32[]{:S(2)}, u32[]{:S(2)}) collective-permute-start(f32[2,3,2,128]{3,2,1,0:T(2,128)S(1)} %get-tuple-element.45), channel_id=1, source_target_pairs={{0,8},{8,16},{16,24},{1,9},{9,17},{17,25},{2,10},{10,18},{18,26},{... | collective-permute-start | bytes 18440 | tf_op jit(solution)/shard_map/ppermute | solution.py:17
  75.5 3.4 %collective-permute-start.11 = (f32[2,3,2,128]{3,2,1,0:T(2,128)S(1)}, f32[2,3,2,128]{3,2,1,0:T(2,128)S(1)}, u32[]{:S(2)}, u32[]{:S(2)}) collective-permute-start(f32[2,3,2,128]{3,2,1,0:T(2,128)S(1)} %get-tuple-element.46), channel_id=1, source_target_pairs={{8,0},{16,8},{24,16},{9,1},{17,9},{25,17},{10,2},{18,10},{26,18},{... | collective-permute-start | bytes 18440 | tf_op jit(solution)/shard_map/ppermute | solution.py:19
  78.9 14.5 %all_gather.7 = f32[2,3,2,1024]{3,2,1,0:T(2,128)S(1)} all-gather(f32[2,3,2,128]{3,2,1,0:T(2,128)S(1)} %pad_maximum_fusion.15), channel_id=1, replica_groups=mesh['lat'=4,'lon'=8] {'lon'}, dimensions={3}, use_global_device_ids=true | all-gather | bytes 55296 | tf_op jit(solution)/shard_map/all_gather | solution.py:75
  93.4 2.4 %copy.239 = f32[2,3,2,1024]{1,2,3,0:T(2,128)} copy(f32[2,3,2,1024]{3,2,1,0:T(2,128)S(1)} %all_gather.7) | data formatting | bytes 98304 | tf_op jit(solution)/shard_map/all_gather | solution.py:75
  95.8 2.6 %gather_fusion.1 = f32[128,2,3,2]{2,3,1,0:T(2,128)S(1)} fusion(f32[2,3,2,1024]{1,2,3,0:T(2,128)} %copy.239, s32[1024]{0:T(1024)} %copy-done.37), kind=kCustom, calls=%fused_computation.1.clone | custom fusion | bytes 12800 | tf_op jit(solution)/shard_map/jit(_take)/gather | solution.py:77
  98.7 1.7 %subtract_multiply_fusion = f32[2,3,257,128]{3,2,1,0:T(8,128)S(1)} fusion(f32[2,3,260,128]{3,2,1,0:T(8,128)S(1)} %fusion.9, f32[3,257,128]{2,1,0:T(8,128)} %get-tuple-element.36, f32[3,257,128]{2,1,0:T(8,128)S(1)} %copy-done.7, f32[3,257,128]{2,1,0:T(8,128)} %copy-done.8, f32[3,257,128]{2,1,0:T(8,128)S(1)} %maximum_multiply_fusion), kind=kLoop, calls=%fused_computation.5 | loop fusion | flops 3158016 | bytes 5526528 | tf_op jit(solution)/shard_map/mul | solution.py:29
  100.5 1.2 %copy.237 = f32[2,3,256,1]{3,2,1,0:T(8,128)} copy(f32[2,3,256,1]{2,3,1,0:T(1,128)S(1)} %get-tuple-element.61) | data formatting | bytes 12288 | tf_op jit(solution)/shard_map/slice | solution.py:87
  102.6 1.2 %copy.233 = f32[2,3,256,1]{3,2,1,0:T(8,128)} copy(f32[2,3,256,1]{2,3,1,0:T(1,128)S(1)} %slice.373) | data formatting | bytes 12288 | tf_op jit(solution)/shard_map/slice | solution.py:83
  103.8 2.8 %subtract_multiply_fusion.2 = f32[2,3,256,1]{3,2,1,0:T(8,128)} fusion(f32[2,3,256,1]{3,2,1,0:T(8,128)} %copy.237, f32[2,3,256,1]{3,2,1,0:T(8,128)S(1)} %copy.242, f32[2,3,256,128]{3,2,1,0:T(8,128)S(1)} %fusion.3, f32[3,256]{1,0:T(4,128)S(1)} %copy-done.31, f32[3,256]{1,0:T(4,128)S(1)} %copy-done.29, f32[3,256]{1,0:T(4,128)S(1)} %copy-done.33, ...), kind=kLoop, calls=%fused_computation.23 | loop fusion | flops 24576 | bytes 43008 | tf_op jit(solution)/shard_map/mul | solution.py:29
  106.6 1.2 %copy.236 = f32[2,3,256,2]{3,2,1,0:T(8,128)} copy(f32[2,3,256,2]{2,3,1,0:T(2,128)S(1)} %copy-done.36) | data formatting | bytes 24576 | tf_op jit(solution)/shard_map/ppermute | solution.py:19
  107.8 3.3 %subtract_multiply_fusion.3 = f32[2,3,256,128]{3,2,1,0:T(8,128)S(1)} fusion(f32[2,3,256,128]{3,2,1,0:T(8,128)S(1)} %fusion.3, f32[2,3,256,2]{3,2,1,0:T(8,128)} %copy.236, f32[2,3,256,126]{3,2,1,0:T(8,128)} %slice.377, f32[2,3,256,127]{3,2,1,0:T(8,128)} %get-tuple-element.40, f32[2,3,256,1]{3,2,1,0:T(8,128)S(1)} %copy.242, f32[2,3,256,1]{3,2,1,0:T(8,128)} %copy.233, ...), kind=kLoop, calls=%fused_computation.24 | loop fusion | flops 3735552 | bytes 5505024 | tf_op jit(solution)/shard_map/mul | solution.py:29
  111.0 1.2 %fusion.1 = f32[2,3,256,128]{3,2,1,0:T(8,128)} fusion(f32[2,3,257,128]{3,2,1,0:T(8,128)S(1)} %subtract_multiply_fusion, f32[2,3,256,128]{3,2,1,0:T(8,128)S(1)} %fusion.3, f32[2,3,256,128]{3,2,1,0:T(8,128)S(1)} %subtract_multiply_fusion.3, f32[2,3,256,127]{3,2,1,0:T(8,128)S(1)} %bitcast.20, f32[2,3,256,1]{3,2,1,0:T(8,128)S(1)} %copy-done.18, ...), kind=kLoop, calls=%fused_computation.9 | loop fusion | flops 1179648 | bytes 5111808 | tf_op jit(solution)/shard_map/mul | solution.py:105
  (138 shorter events, 5.4 us)
Async XLA Ops:
  0.0 8.8 %copy-start.14 = (f32[3,256,128]{2,1,0:T(8,128)S(1)}, f32[3,256,128]{2,1,0:T(8,128)}, u32[]{:S(2)}) copy-start(f32[3,256,128]{2,1,0:T(8,128)} %param.14) | copy-start | bytes 1179652
  0.0 9.6 %copy-start.24 = (f32[3,256,128]{2,1,0:T(8,128)S(1)}, f32[3,256,128]{2,1,0:T(8,128)}, u32[]{:S(2)}) copy-start(f32[3,256,128]{2,1,0:T(8,128)} %param.15) | copy-start | bytes 1179652
  1.1 8.5 %copy-start.11 = (f32[3,256,128]{2,1,0:T(8,128)S(1)}, f32[3,256,128]{2,1,0:T(8,128)}, u32[]{:S(2)}) copy-start(f32[3,256,128]{2,1,0:T(8,128)} %param.16) | copy-start | bytes 1179652
  1.1 8.6 %copy-start.25 = (f32[3,256,128]{2,1,0:T(8,128)S(1)}, f32[3,256,128]{2,1,0:T(8,128)}, u32[]{:S(2)}) copy-start(f32[3,256,128]{2,1,0:T(8,128)} %param.17) | copy-start | bytes 1179652
  2.4 7.3 %copy-start.13 = (s32[3,256,128]{2,1,0:T(8,128)S(1)}, s32[3,256,128]{2,1,0:T(8,128)}, u32[]{:S(2)}) copy-start(s32[3,256,128]{2,1,0:T(8,128)} %param.18) | copy-start | bytes 1179652
  2.4 30.4 %collective-permute-start.7 = (f32[2,3,2,128]{3,2,1,0:T(2,128)S(1)}, f32[2,3,2,128]{3,2,1,0:T(2,128)S(1)}, u32[]{:S(2)}, u32[]{:S(2)}) collective-permute-start(f32[2,3,2,128]{3,2,1,0:T(2,128)S(1)} %get-tuple-element.54), channel_id=1, source_target_pairs={{8,0},{16,8},{24,16},{9,1},{17,9},{25,17},{10,2},{18,10},{26,18},{... | collective-permute-start | bytes 18440 | tf_op jit(solution)/shard_map/ppermute | solution.py:19
  4.7 28.3 %collective-permute-start.6 = (f32[2,3,2,128]{3,2,1,0:T(2,128)S(1)}, f32[2,3,2,128]{3,2,1,0:T(2,128)S(1)}, u32[]{:S(2)}, u32[]{:S(2)}) collective-permute-start(f32[2,3,2,128]{3,2,1,0:T(2,128)S(1)} %get-tuple-element.53), channel_id=1, source_target_pairs={{0,8},{8,16},{16,24},{1,9},{9,17},{17,25},{2,10},{10,18},{18,26},{... | collective-permute-start | bytes 18440 | tf_op jit(solution)/shard_map/ppermute | solution.py:17
  11.1 22.1 %collective-permute-start.1 = (f32[15,1,128]{2,0,1:T(8,128)S(1)}, f32[15,1,128]{2,0,1:T(8,128)S(1)}, u32[]{:S(2)}, u32[]{:S(2)}) collective-permute-start(f32[15,1,128]{2,0,1:T(8,128)S(1)} %copy.213), channel_id=1, source_target_pairs={{8,0},{16,8},{24,16},{0,24},{9,1},{17,9},{25,17},{1,25},{10,2},{18... | collective-permute-start | bytes 23048 | tf_op jit(solution)/shard_map/ppermute | solution.py:19
  11.2 22.1 %collective-permute-start = (f32[15,1,128]{2,0,1:T(8,128)S(1)}, f32[15,1,128]{2,0,1:T(8,128)S(1)}, u32[]{:S(2)}, u32[]{:S(2)}) collective-permute-start(f32[15,1,128]{2,0,1:T(8,128)S(1)} %copy.212), channel_id=1, source_target_pairs={{0,8},{8,16},{16,24},{24,0},{1,9},{9,17},{17,25},{25,1},{2,10},{10... | collective-permute-start | bytes 23048 | tf_op jit(solution)/shard_map/ppermute | solution.py:17
  13.8 4.7 %copy-start.42 = (s32[128]{0:T(128)S(1)}, s32[128]{0:T(128)}, u32[]{:S(2)}) copy-start(s32[128]{0:T(128)} %param.19) | copy-start | bytes 1540
  14.1 36.2 %collective-permute-start.4 = (f32[2,3,256,2]{2,3,1,0:T(2,128)S(1)}, f32[2,3,256,2]{2,3,1,0:T(2,128)S(1)}, u32[]{:S(2)}, u32[]{:S(2)}) collective-permute-start(f32[2,3,256,2]{2,3,1,0:T(2,128)S(1)} %copy.220), channel_id=1, source_target_pairs={{0,1},{1,2},{2,3},{3,4},{4,5},{5,6},{6,7},{7,0},{8,9},{9,10},{10,1... | collective-permute-start | bytes 36872 | tf_op jit(solution)/shard_map/ppermute | solution.py:17
  18.5 14.7 %copy-start.38 = (pred[128]{0:T(512)(128)(4,1)}, pred[128]{0:T(512)(128)(4,1)S(1)}, u32[]{:S(2)}) copy-start(pred[128]{0:T(512)(128)(4,1)S(1)} %get-tuple-element.32) | copy-start | bytes 388
  18.5 14.7 %copy-start.40 = (pred[128]{0:T(512)(128)(4,1)}, pred[128]{0:T(512)(128)(4,1)S(1)}, u32[]{:S(2)}) copy-start(pred[128]{0:T(512)(128)(4,1)S(1)} %get-tuple-element.65) | copy-start | bytes 388
  18.5 11.4 %copy-start.37 = (s32[1024]{0:T(1024)}, s32[1024]{0:T(1024)S(1)}, u32[]{:S(2)}) copy-start(s32[1024]{0:T(1024)S(1)} %pad_clamp_fusion) | copy-start | bytes 12292
  32.9 19.9 %collective-permute-start.3 = (f32[2,3,256,2]{2,3,1,0:T(2,128)S(1)}, f32[2,3,256,2]{2,3,1,0:T(2,128)S(1)}, u32[]{:S(2)}, u32[]{:S(2)}) collective-permute-start(f32[2,3,256,2]{2,3,1,0:T(2,128)S(1)} %copy.218), channel_id=1, source_target_pairs={{1,0},{2,1},{3,2},{4,3},{5,4},{6,5},{7,6},{0,7},{9,8},{10,9},{11,1... | collective-permute-start | bytes 36872 | tf_op jit(solution)/shard_map/ppermute | solution.py:19
  33.1 2.2 %copy-start.1 = (f32[15,256,128]{2,1,0:T(8,128)S(1)}, f32[15,256,128]{2,1,0:T(8,128)}, u32[]{:S(2)}) copy-start(f32[15,256,128]{2,1,0:T(8,128)} %copy-done) | copy-start | bytes 5898244
  33.2 2.3 %copy-start.27 = (f32[15,1,128]{2,1,0:T(1,128)}, f32[15,1,128]{2,1,0:T(1,128)S(1)}, u32[]{:S(2)}) copy-start(f32[15,1,128]{2,1,0:T(1,128)S(1)} %copy.215) | copy-start | bytes 23044
  33.3 2.3 %copy-start.26 = (f32[15,1,128]{2,1,0:T(1,128)}, f32[15,1,128]{2,1,0:T(1,128)S(1)}, u32[]{:S(2)}) copy-start(f32[15,1,128]{2,1,0:T(1,128)S(1)} %copy.214) | copy-start | bytes 23044
  35.3 12.4 %copy-start.6 = (f32[3,257,128]{2,1,0:T(8,128)}, f32[3,257,128]{2,1,0:T(8,128)S(1)}, u32[]{:S(2)}) copy-start(f32[3,257,128]{2,1,0:T(8,128)S(1)} %get-tuple-element.30) | copy-start | bytes 1184260
  35.4 12.4 %copy-start.8 = (f32[3,257,128]{2,1,0:T(8,128)}, f32[3,257,128]{2,1,0:T(8,128)S(1)}, u32[]{:S(2)}) copy-start(f32[3,257,128]{2,1,0:T(8,128)S(1)} %get-tuple-element.31) | copy-start | bytes 1184260
  41.2 15.4 %collective-permute-start.5 = (f32[15,258,1]{1,0,2:T(8,128)}, f32[15,258,1]{1,0,2:T(8,128)}, u32[]{:S(2)}, u32[]{:S(2)}) collective-permute-start(f32[15,258,1]{1,0,2:T(8,128)} %copy.223), channel_id=1, source_target_pairs={{0,1},{1,2},{2,3},{3,4},{4,5},{5,6},{6,7},{7,0},{8,9},{9,10},{10,1... | collective-permute-start | bytes 46448 | tf_op jit(solution)/shard_map/ppermute | solution.py:17
  45.9 14.4 %collective-permute-start.2 = (f32[15,258,1]{1,0,2:T(8,128)}, f32[15,258,1]{1,0,2:T(8,128)}, u32[]{:S(2)}, u32[]{:S(2)}) collective-permute-start(f32[15,258,1]{1,0,2:T(8,128)} %copy.216), channel_id=1, source_target_pairs={{1,0},{2,1},{3,2},{4,3},{5,4},{6,5},{7,6},{0,7},{9,8},{10,9},{11,1... | collective-permute-start | bytes 46448 | tf_op jit(solution)/shard_map/ppermute | solution.py:19
  54.6 8.4 %copy-start.2 = (f32[15,256,128]{2,1,0:T(8,128)S(1)}, f32[15,256,128]{2,1,0:T(8,128)}, u32[]{:S(2)}) copy-start(f32[15,256,128]{2,1,0:T(8,128)} %copy-done) | copy-start | bytes 5898244
  63.0 1.6 %copy-start.3 = (f32[2,3,256,1]{3,2,1,0:T(8,128)S(1)}, f32[2,3,256,1]{3,2,1,0:T(8,128)}, u32[]{:S(2)}) copy-start(f32[2,3,256,1]{3,2,1,0:T(8,128)} %copy.241) | copy-start | bytes 18436
  63.0 1.6 %copy-start.17 = (f32[2,3,256,1]{3,2,1,0:T(8,128)S(1)}, f32[2,3,256,1]{3,2,1,0:T(8,128)}, u32[]{:S(2)}) copy-start(f32[2,3,256,1]{3,2,1,0:T(8,128)} %copy.225) | copy-start | bytes 18436
  63.0 1.6 %copy-start.28 = (f32[3,256]{1,0:T(4,128)S(1)}, f32[3,256]{1,0:T(4,128)}, u32[]{:S(2)}) copy-start(f32[3,256]{1,0:T(4,128)} %get-tuple-element.58) | copy-start | bytes 9220
  63.0 1.7 %copy-start.30 = (f32[3,256]{1,0:T(4,128)S(1)}, f32[3,256]{1,0:T(4,128)}, u32[]{:S(2)}) copy-start(f32[3,256]{1,0:T(4,128)} %get-tuple-element.59) | copy-start | bytes 9220
  63.0 1.7 %copy-start.32 = (f32[3,256]{1,0:T(4,128)S(1)}, f32[3,256]{1,0:T(4,128)}, u32[]{:S(2)}) copy-start(f32[3,256]{1,0:T(4,128)} %get-tuple-element.60) | copy-start | bytes 9220
  63.0 2.4 %copy-start.21 = (f32[2,3,256,2]{3,2,1,0:T(8,128)S(1)}, f32[2,3,256,2]{3,2,1,0:T(8,128)}, u32[]{:S(2)}) copy-start(f32[2,3,256,2]{3,2,1,0:T(8,128)} %copy.222) | copy-start | bytes 36868
  63.0 2.4 %copy-start.22 = (f32[2,3,256,127]{3,2,1,0:T(8,128)S(1)}, f32[2,3,256,127]{3,2,1,0:T(8,128)}, u32[]{:S(2)}) copy-start(f32[2,3,256,127]{3,2,1,0:T(8,128)} %get-tuple-element.47) | copy-start | bytes 2340868
  63.0 2.4 %copy-start.23 = (f32[2,3,256,127]{3,2,1,0:T(8,128)S(1)}, f32[2,3,256,127]{3,2,1,0:T(8,128)}, u32[]{:S(2)}) copy-start(f32[2,3,256,127]{3,2,1,0:T(8,128)} %get-tuple-element.48) | copy-start | bytes 2340868
  64.7 1.6 %copy-start.15 = (f32[3,256,128]{2,1,0:T(8,128)S(1)}, f32[3,256,128]{2,1,0:T(8,128)}, u32[]{:S(2)}) copy-start(f32[3,256,128]{2,1,0:T(8,128)} %param.14) | copy-start | bytes 1179652
  64.7 1.7 %copy-start.16 = (f32[3,256,128]{2,1,0:T(8,128)S(1)}, f32[3,256,128]{2,1,0:T(8,128)}, u32[]{:S(2)}) copy-start(f32[3,256,128]{2,1,0:T(8,128)} %get-tuple-element.55) | copy-start | bytes 1179652
  64.7 1.9 %copy-start.19 = (f32[2,3,256,126]{3,2,1,0:T(8,128)S(1)}, f32[2,3,256,126]{3,2,1,0:T(8,128)}, u32[]{:S(2)}) copy-start(f32[2,3,256,126]{3,2,1,0:T(8,128)} %slice.348) | copy-start | bytes 2322436
  64.7 2.2 %copy-start.20 = (f32[2,3,256,1]{3,2,1,0:T(8,128)S(1)}, f32[2,3,256,1]{3,2,1,0:T(8,128)}, u32[]{:S(2)}) copy-start(f32[2,3,256,1]{3,2,1,0:T(8,128)} %copy.219) | copy-start | bytes 18436
  71.6 28.9 %collective-permute-start.9 = (f32[2,3,256,2]{2,3,1,0:T(2,128)S(1)}, f32[2,3,256,2]{2,3,1,0:T(2,128)S(1)}, u32[]{:S(2)}, u32[]{:S(2)}) collective-permute-start(f32[2,3,256,2]{2,3,1,0:T(2,128)S(1)} %copy.234), channel_id=1, source_target_pairs={{0,1},{1,2},{2,3},{3,4},{4,5},{5,6},{6,7},{7,0},{8,9},{9,10},{10,1... | collective-permute-start | bytes 36872 | tf_op jit(solution)/shard_map/ppermute | solution.py:17
  71.8 30.1 %collective-permute-start.8 = (f32[2,3,256,2]{2,3,1,0:T(2,128)S(1)}, f32[2,3,256,2]{2,3,1,0:T(2,128)S(1)}, u32[]{:S(2)}, u32[]{:S(2)}) collective-permute-start(f32[2,3,256,2]{2,3,1,0:T(2,128)S(1)} %copy.232), channel_id=1, source_target_pairs={{1,0},{2,1},{3,2},{4,3},{5,4},{6,5},{7,6},{0,7},{9,8},{10,9},{11,1... | collective-permute-start | bytes 36872 | tf_op jit(solution)/shard_map/ppermute | solution.py:19
  73.6 25.0 %collective-permute-start.10 = (f32[2,3,2,128]{3,2,1,0:T(2,128)S(1)}, f32[2,3,2,128]{3,2,1,0:T(2,128)S(1)}, u32[]{:S(2)}, u32[]{:S(2)}) collective-permute-start(f32[2,3,2,128]{3,2,1,0:T(2,128)S(1)} %get-tuple-element.45), channel_id=1, source_target_pairs={{0,8},{8,16},{16,24},{1,9},{9,17},{17,25},{2,10},{10,18},{18,26},{... | collective-permute-start | bytes 18440 | tf_op jit(solution)/shard_map/ppermute | solution.py:17
  75.5 23.1 %collective-permute-start.11 = (f32[2,3,2,128]{3,2,1,0:T(2,128)S(1)}, f32[2,3,2,128]{3,2,1,0:T(2,128)S(1)}, u32[]{:S(2)}, u32[]{:S(2)}) collective-permute-start(f32[2,3,2,128]{3,2,1,0:T(2,128)S(1)} %get-tuple-element.46), channel_id=1, source_target_pairs={{8,0},{16,8},{24,16},{9,1},{17,9},{25,17},{10,2},{18,10},{26,18},{... | collective-permute-start | bytes 18440 | tf_op jit(solution)/shard_map/ppermute | solution.py:19
  93.4 5.3 %copy-start.39 = (pred[128]{0:T(512)(128)(4,1)S(1)}, pred[128]{0:T(512)(128)(4,1)}, u32[]{:S(2)}) copy-start(pred[128]{0:T(512)(128)(4,1)} %copy-done.38) | copy-start | bytes 388
  93.4 5.3 %copy-start.41 = (pred[128]{0:T(512)(128)(4,1)S(1)}, pred[128]{0:T(512)(128)(4,1)}, u32[]{:S(2)}) copy-start(pred[128]{0:T(512)(128)(4,1)} %copy-done.40) | copy-start | bytes 388
  93.4 5.3 %copy-start.7 = (f32[3,257,128]{2,1,0:T(8,128)S(1)}, f32[3,257,128]{2,1,0:T(8,128)}, u32[]{:S(2)}) copy-start(f32[3,257,128]{2,1,0:T(8,128)} %copy-done.6) | copy-start | bytes 1184260
  100.4 3.3 %copy-start.29 = (f32[3,256]{1,0:T(4,128)S(1)}, f32[3,256]{1,0:T(4,128)}, u32[]{:S(2)}) copy-start(f32[3,256]{1,0:T(4,128)} %get-tuple-element.58) | copy-start | bytes 9220
  100.5 3.3 %copy-start.31 = (f32[3,256]{1,0:T(4,128)S(1)}, f32[3,256]{1,0:T(4,128)}, u32[]{:S(2)}) copy-start(f32[3,256]{1,0:T(4,128)} %get-tuple-element.59) | copy-start | bytes 9220
  100.5 3.3 %copy-start.33 = (f32[3,256]{1,0:T(4,128)S(1)}, f32[3,256]{1,0:T(4,128)}, u32[]{:S(2)}) copy-start(f32[3,256]{1,0:T(4,128)} %get-tuple-element.60) | copy-start | bytes 9220
  103.8 2.8 %copy-start.36 = (f32[2,3,256,2]{2,3,1,0:T(2,128)S(1)}, f32[2,3,256,2]{2,3,1,0:T(2,128)}, u32[]{:S(2)}) copy-start(f32[2,3,256,2]{2,3,1,0:T(2,128)} %copy-done.35) | copy-start | bytes 36868
  103.8 4.0 %copy-start.10 = (f32[3,256,128]{2,1,0:T(8,128)S(1)}, f32[3,256,128]{2,1,0:T(8,128)}, u32[]{:S(2)}) copy-start(f32[3,256,128]{2,1,0:T(8,128)} %copy-done.9) | copy-start | bytes 1179652
  107.8 3.3 %copy-start.18 = (f32[2,3,256,1]{3,2,1,0:T(8,128)S(1)}, f32[2,3,256,1]{3,2,1,0:T(8,128)}, u32[]{:S(2)}) copy-start(f32[2,3,256,1]{3,2,1,0:T(8,128)} %subtract_multiply_fusion.2) | copy-start | bytes 18436
  (7 other events, 7.4 us)
where the time goes:
time: 113 us; the launch traced here: 112 us
  local copies, waits for them, and re-layouts  43.5 us (38%)
  other arithmetic  23.2 us (21%)
  starting transfers between devices  22.4 us (20%)
  blocking collectives  22.4 us (20%)
    all_gather x2, blocking collectives, local(): piece = lax.all_gather(top, 'lon', axis=3, tiled=True)  22.4 us
    ppermute x6, starting transfers between devices, extended(): lax.ppermute(tail, axis, [(i, (i + 1) % count) for i in range(ends)])  12.9 us
    mul x6, other arithmetic, face_flux(): opened * (courant * centered / 12.0 - jnp.abs(courant) * upwind / 12.0 -...  11.7 us
    ppermute x6, starting transfers between devices, extended(): lax.ppermute(head, axis, [((i + 1) % count, i) for i in range(ends)])  9.49 us
    unnamed x91, local copies, waits for them, and re-layouts  6 us
    ppermute x4, local copies, waits for them, and re-layouts, extended(): lax.ppermute(head, axis, [((i + 1) % count, i) for i in range(ends)])  5.89 us
    slice x5, local copies, waits for them, and re-layouts, extended(): lax.slice_in_dim(cells, cells.shape[dim] - width, cells.shape[dim], axis=...  5.7 us
    gather x4, local copies, waits for them, and re-layouts, local(): picked = jnp.take(piece, jnp.clip(fold_map, 0, piece.shape[3] - 1), axis=3)  5.52 us
  transfers between devices with their start and end apart: 12, of which 0 were waited for; matrix products, arithmetic and copies ran while one was open for 37% of the time, Pallas kernels for 0%

commit v1 on v0

v1 whole, which is shorter than its diff:
```python
import functools

import jax
import jax.numpy as jnp
from jax import lax
from jax.experimental import pallas as pl
from jax.experimental.pallas import tpu as pltpu
from jax.sharding import PartitionSpec as P

MESH = pl.DeviceIdType.MESH
F32 = jnp.float32
TOP = 16
BLOCK = 64


def face_flux(behind, center, forward, beyond, courant, diffusivity, opened):
    centered = 7.0 * (center + forward) - (behind + beyond)
    upwind = 3.0 * (forward - center) - (beyond - behind)
    return opened * (
        courant * centered * (1.0 / 12.0)
        - jnp.abs(courant) * upwind * (1.0 / 12.0)
        - diffusivity * (forward - center)
    )


def face_weights(courant, diffusivity, opened):
    ahead = courant >= 0.0
    scaled = opened * courant * (1.0 / 6.0)
    spread = opened * diffusivity
    center = scaled * jnp.where(ahead, 5.0, 2.0) + spread
    forward = scaled * jnp.where(ahead, 2.0, 5.0) - spread
    return ahead, center, forward, -scaled


def reversed_lanes(values):
    lane = lax.broadcasted_iota(jnp.int32, values.shape, values.ndim - 1)
    axis = values.ndim - 1
    step = values.shape[-1] // 2
    while step:
        up = pltpu.roll(values, values.shape[-1] - step, axis)
        down = pltpu.roll(values, step, axis)
        values = jnp.where((lane & step) == 0, up, down)
        step //= 2
    return values


def kernel(
    nlat, nlon, fold_ref, tr, ec, nc, ek, nk, mask, out,
    s0, s1, ocean, we, wn, packed, t0, t1, ct, ce,
    se, sw, sn, ss, sf, re, rw, rn, rs, rf0, rf1, north_rows,
    send_sem, recv_sem, fold_send, fold_recv,
):
    levels, rows, cols = mask.shape
    lat = lax.axis_index("lat")
    lon = lax.axis_index("lon")
    southern = lat == 0
    northern = lat == nlat - 1
    east = lax.rem(lon + 1, nlon)
    west = lax.rem(lon + nlon - 1, nlon)
    barrier = pltpu.get_barrier_semaphore()
    rf = (rf0, rf1)

    def greet(a, b):
        pl.semaphore_signal(barrier, inc=1, device_id=(a, b), device_id_type=MESH)

    greet(lat, east)
    greet(lat, west)

    @pl.when(jnp.logical_not(southern))
    def _():
        greet(lat - 1, lon)

    @pl.when(jnp.logical_not(northern))
    def _():
        greet(lat + 1, lon)

    @pl.when(northern)
    def _():
        for d in range(2, nlon - 1):
            greet(lat, lax.rem(lon + d, nlon))

    lane = lax.broadcasted_iota(jnp.int32, (BLOCK, cols), 1)
    starts = range(0, rows, BLOCK)

    def level_setup(l, carry):
        for r in starts:
            o = mask[l, r : r + BLOCK, :].astype(F32)
            ocean[l, r : r + BLOCK, :] = o
            for t in range(2):
                s0[t * levels + l, TOP + r : TOP + r + BLOCK, :] = tr[t, l, r : r + BLOCK, :] * o
        ocean[l, rows : rows + 8, :] = jnp.zeros((8, cols), F32)
        for t in range(2):
            for s in (s0, s1):
                s[t * levels + l, 0:TOP, :] = jnp.zeros((TOP, cols), F32)
                s[t * levels + l, TOP + rows : TOP + rows + 8, :] = jnp.zeros((8, cols), F32)
        wn[0, l, 0:8, :] = jnp.zeros((8, cols), F32)
        wn[1, l, 0:8, :] = jnp.zeros((8, cols), F32)
        wn[2, l, 0:8, :] = jnp.zeros((8, cols), F32)
        return carry

    lax.fori_loop(0, levels, level_setup, 0)

    def row(s, r):
        return s[:, TOP + r : TOP + r + 1, :]

    def remote(src, dst, step, which, a, b):
        return pltpu.make_async_remote_copy(
            src_ref=src, dst_ref=dst, send_sem=send_sem.at[step, which],
            recv_sem=recv_sem.at[step, which], device_id=(a, b), device_id_type=MESH,
        )

    def to_east(step):
        return remote(se.at[step], rw.at[step], step, 0, lat, east)

    def to_west(step):
        return remote(sw.at[step], re.at[step], step, 1, lat, west)

    def to_north(step):
        return remote(sn.at[step], rs.at[step], step, 2, lat + 1, lon)

    def to_south(step):
        return remote(ss.at[step], rn.at[step], step, 3, lat - 1, lon)

    def to_fold(step, d):
        return pltpu.make_async_remote_copy(
            src_ref=sf.at[step], dst_ref=rf[step].at[lon], send_sem=fold_send.at[step, d - 1],
            recv_sem=fold_recv.at[step, d - 1], device_id=(lat, lax.rem(lon + d, nlon)),
            device_id_type=MESH,
        )

    def start_lat(step):
        @pl.when(jnp.logical_not(northern))
        def _():
            to_north(step).start()

        @pl.when(jnp.logical_not(southern))
        def _():
            to_south(step).start()

        @pl.when(northern)
        def _():
            for d in range(1, nlon):
                to_fold(step, d).start()

    def wait_lat(step):
        @pl.when(jnp.logical_not(northern))
        def _():
            to_north(step).wait_send()
            to_south(step).wait_recv()

        @pl.when(jnp.logical_not(southern))
        def _():
            to_south(step).wait_send()
            to_north(step).wait_recv()

        @pl.when(northern)
        def _():
            for d in range(1, nlon):
                to_fold(step, d).wait()

    def fill_rows(step, s):
        sn[step, 0:6] = row(s, rows - 2)
        sn[step, 6:12] = row(s, rows - 1)
        ss[step, 0:6] = row(s, 0)
        ss[step, 6:12] = row(s, 1)
        sf[step, 0:6] = row(s, rows - 1)
        sf[step, 6:12] = row(s, rows - 2)
        rf[step][lon] = sf[step]

    fill_rows(0, s0)
    sn[0, 12:15] = nc[:, rows - 1 : rows, :]
    sn[0, 15:18] = nk[:, rows - 1 : rows, :]
    sn[0, 18:21] = ocean[:, rows - 1 : rows, :]
    ss[0, 12:15] = ocean[:, 0:1, :]

    @pl.when(northern)
    def _():
        pl.semaphore_wait(barrier, nlon)

    @pl.when(southern)
    def _():
        pl.semaphore_wait(barrier, 3)

    @pl.when(jnp.logical_not(northern | southern))
    def _():
        pl.semaphore_wait(barrier, 4)

    start_lat(0)

    def pack(fields, target):
        for r in starts:
            acc = jnp.zeros((BLOCK, cols), F32)
            for k, (ref, index, base) in enumerate(fields):
                x = ref[index, base + r : base + r + BLOCK, :]
                acc = jnp.where(lane // 4 == k, pltpu.roll(x, (4 * k + 2) % cols, 1), acc)
            packed[r : r + BLOCK, :] = acc
        for h in range(rows // cols):
            target[h] = packed[h * cols : (h + 1) * cols, :].T

    halves = range(rows // cols)

    def column(ref, h, j, first, count):
        return ref[h, pl.ds(4 * first + j, count, stride=4), :]

    fields = [(s0, f, TOP) for f in range(2 * levels)]
    for ref in (ocean, ec, ek):
        fields += [(ref, l, 0) for l in range(levels)]
    pack(fields, t0)
    n = 2 * levels
    for h in halves:
        se[0, h, 0:n] = column(t0, h, 0, 0, n)
        se[0, h, n : 2 * n] = column(t0, h, 1, 0, n)
        for i in range(3):
            at = 2 * n + i * levels
            se[0, h, at : at + levels] = column(t0, h, 1, n + i * levels, levels)
        sw[0, h, 0:n] = column(t0, h, 2, 0, n)
        sw[0, h, n : 2 * n] = column(t0, h, 3, 0, n)
        sw[0, h, 2 * n : 2 * n + levels] = column(t0, h, 2, n, levels)
    to_east(0).start()
    to_west(0).start()

    def level_weights(l, carry):
        for r in starts:
            o = ocean[l, r : r + BLOCK, :]
            u = ec[l, r : r + BLOCK, :]
            opened = jnp.where(lane == cols - 1, 0.0, o * pltpu.roll(o, cols - 1, 1))
            ahead, center, forward, far = face_weights(u, ek[l, r : r + BLOCK, :], opened)
            outside = ((lane == 0) & ahead) | ((lane == cols - 2) & jnp.logical_not(ahead))
            we[0, l, r : r + BLOCK, :] = center
            we[1, l, r : r + BLOCK, :] = forward
            we[2, l, r : r + BLOCK, :] = jnp.where(outside, 0.0, far)
            u = nc[l, r : r + BLOCK, :]
            opened = o * ocean[l, r + 1 : r + 1 + BLOCK, :]
            ahead, center, forward, far = face_weights(u, nk[l, r : r + BLOCK, :], opened)
            wn[0, l, 8 + r : 8 + r + BLOCK, :] = center
            wn[1, l, 8 + r : 8 + r + BLOCK, :] = forward
            wn[2, l, 8 + r : 8 + r + BLOCK, :] = far
        return carry

    lax.fori_loop(0, levels, level_weights, 0)

    def advance(s, put):
        def level(l, carry):
            for r in starts:
                ea = we[0, l, r : r + BLOCK, :]
                eb = we[1, l, r : r + BLOCK, :]
                ee = we[2, l, r : r + BLOCK, :]
                na = wn[0, l, r : r + BLOCK + 8, :]
                nb = wn[1, l, r : r + BLOCK + 8, :]
                ne = wn[2, l, r : r + BLOCK + 8, :]
                o = ocean[l, r : r + BLOCK, :]
                for t in range(2):
                    f = t * levels + l
                    base = TOP + r
                    q = s[f, base : base + BLOCK, :]
                    far = jnp.where(ee <= 0.0, pltpu.roll(q, 1, 1), pltpu.roll(q, cols - 2, 1))
                    flux = ea * q + eb * pltpu.roll(q, cols - 1, 1) + ee * far
                    total = q - flux + pltpu.roll(flux, 1, 1)
                    b = s[f, base - 8 : base + BLOCK, :]
                    a = s[f, base - 9 : base + BLOCK - 1, :]
                    c = s[f, base - 7 : base + BLOCK + 1, :]
                    d = s[f, base - 6 : base + BLOCK + 2, :]
                    flux = na * b + nb * c + ne * jnp.where(ne <= 0.0, a, d)
                    total = total - flux[8:] + flux[7 : 7 + BLOCK]
                    put(t, l, r, o * total)
            return carry

        lax.fori_loop(0, levels, level, 0)

    def put_s1(t, l, r, value):
        s1[t * levels + l, TOP + r : TOP + r + BLOCK, :] = value

    def put_out(t, l, r, value):
        out[t, l, r : r + BLOCK, :] = value

    def rows_fixed(step, s, add):
        @pl.when(northern)
        def _():
            picked = rf[step][lax.div(fold_ref[0], jnp.int32(cols))]
            north_rows[...] = reversed_lanes(picked)

        @pl.when(jnp.logical_not(northern))
        def _():
            north_rows[...] = rn[step, 0:12]

        o0, o1 = ocean[:, 0:1, :], ocean[:, 1:2, :]
        oy, oz = ocean[:, rows - 2 : rows - 1, :], ocean[:, rows - 1 : rows, :]
        above = jnp.where(northern, oz, rn[0, 12:15])
        below = jnp.where(southern, 0.0, rs[0, 18:21])
        first = o0 * o1 * jnp.maximum(nc[:, 0:1, :], 0.0) * (-1.0 / 6.0)
        last = oy * oz * jnp.minimum(nc[:, rows - 2 : rows - 1, :], 0.0) * (-1.0 / 6.0)
        for t in range(2):
            part = slice(t * levels, (t + 1) * levels)
            part2 = slice((2 + t) * levels, (3 + t) * levels)
            q0, q1 = s[part, TOP : TOP + 1, :], s[part, TOP + 1 : TOP + 2, :]
            qy = s[part, TOP + rows - 2 : TOP + rows - 1, :]
            qz = s[part, TOP + rows - 1 : TOP + rows, :]
            m2 = jnp.where(southern, 0.0, rs[step, part])
            m1 = jnp.where(southern, 0.0, rs[step, part2])
            p0, p1 = north_rows[part], north_rows[part2]
            low = face_flux(
                m2, m1, q0, q1, jnp.where(southern, 0.0, rs[0, 12:15]),
                jnp.where(southern, 0.0, rs[0, 15:18]), below * o0,
            )
            high = face_flux(
                qy, qz, p0, p1, nc[:, rows - 1 : rows, :], nk[:, rows - 1 : rows, :], oz * above
            )
            enters = first * m1
            leaves = last * p0
            add(t, 0, o0 * (low - enters))
            add(t, 1, o1 * enters)
            add(t, rows - 2, -oy * leaves)
            add(t, rows - 1, oz * (leaves - high))

    def columns_fixed(step, tq):
        for h in halves:
            oy, oz, o0, o1 = [column(t0, h, j, n, levels) for j in range(4)]
            cy, cz, c0, _ = [column(t0, h, j, n + levels, levels) for j in range(4)]
            kz = column(t0, h, 1, n + 2 * levels, levels)
            om = rw[0, h, 2 * n : 2 * n + levels]
            cm = rw[0, h, 2 * n + levels : 2 * n + 2 * levels]
            km = rw[0, h, 2 * n + 2 * levels : 2 * n + 3 * levels]
            op = re[0, h, 2 * n : 2 * n + levels]
            first = o0 * o1 * jnp.maximum(c0, 0.0) * (-1.0 / 6.0)
            last = oy * oz * jnp.minimum(cy, 0.0) * (-1.0 / 6.0)
            for t in range(2):
                qy, qz, q0, q1 = [column(tq, h, j, t * levels, levels) for j in range(4)]
                m2 = rw[step, h, t * levels : (t + 1) * levels]
                m1 = rw[step, h, n + t * levels : n + (t + 1) * levels]
                p0 = re[step, h, t * levels : (t + 1) * levels]
                p1 = re[step, h, n + t * levels : n + (t + 1) * levels]
                low = face_flux(m2, m1, q0, q1, cm, km, om * o0)
                high = face_flux(qy, qz, p0, p1, cz, kz, oz * op)
                enters = first * m1
                leaves = last * p0
                for j, fix in enumerate(
                    (-oy * leaves, oz * (leaves - high), o0 * (low - enters), o1 * enters)
                ):
                    ct[h, pl.ds(4 * t * levels + j, levels, stride=4), :] = fix

    def spread_columns(add):
        edge = (lane < 2) | (lane >= cols - 2)
        for h in halves:
            ce[h * cols : (h + 1) * cols, :] = ct[h].T
        for r in starts:
            x = ce[r : r + BLOCK, :]
            for f in range(n):
                add(f, r, jnp.where(edge, pltpu.roll(x, (cols - 4 * f - 2) % cols, 1), 0.0))

    advance(s0, put_s1)
    for h in halves:
        ct[h] = jnp.zeros((cols, cols), F32)
    wait_lat(0)
    to_east(0).wait()
    to_west(0).wait()

    def add_row_s1(t, r, value):
        part = slice(t * levels, (t + 1) * levels)
        s1[part, TOP + r : TOP + r + 1, :] = s1[part, TOP + r : TOP + r + 1, :] + value

    rows_fixed(0, s0, add_row_s1)
    columns_fixed(0, t0)
    pack([(s1, f, TOP) for f in range(n)], t1)
    for h in halves:
        t1[h, 0 : 4 * n] = t1[h, 0 : 4 * n] + ct[h, 0 : 4 * n]
        se[1, h, 0:n] = column(t1, h, 0, 0, n)
        se[1, h, n : 2 * n] = column(t1, h, 1, 0, n)
        sw[1, h, 0:n] = column(t1, h, 2, 0, n)
        sw[1, h, n : 2 * n] = column(t1, h, 3, 0, n)
    to_east(1).start()
    to_west(1).start()

    def add_s1(f, r, value):
        at = slice(TOP + r, TOP + r + BLOCK)
        s1[f, at, :] = s1[f, at, :] + value

    spread_columns(add_s1)
    fill_rows(1, s1)
    start_lat(1)
    advance(s1, put_out)
    wait_lat(1)
    to_east(1).wait()
    to_west(1).wait()

    def add_row_out(t, r, value):
        out[t, :, r : r + 1, :] = out[t, :, r : r + 1, :] + value

    rows_fixed(1, s1, add_row_out)
    columns_fixed(1, t1)

    def add_out(f, r, value):
        t, l = divmod(f, levels)
        out[t, l, r : r + BLOCK, :] = out[t, l, r : r + BLOCK, :] + value

    spread_columns(add_out)


def local(tracers, east_courant, north_courant, east_kappa, north_kappa, ocean_mask, fold_map):
    nlat = lax.axis_size("lat")
    nlon = lax.axis_size("lon")
    levels, rows, cols = ocean_mask.shape
    fields = 2 * levels
    halves = rows // cols

    def scratch(*shape):
        return pltpu.VMEM(shape, F32)

    whole = pl.BlockSpec(memory_space=pltpu.VMEM)
    return pl.pallas_call(
        functools.partial(kernel, nlat, nlon),
        out_shape=jax.ShapeDtypeStruct(tracers.shape, F32),
        in_specs=[pl.BlockSpec(memory_space=pltpu.SMEM)] + [whole] * 6,
        out_specs=whole,
        scratch_shapes=[
            scratch(fields, TOP + rows + 8, cols),
            scratch(fields, TOP + rows + 8, cols),
            scratch(levels, rows + 8, cols),
            scratch(3, levels, rows, cols),
            scratch(3, levels, rows + 8, cols),
            scratch(rows, cols),
            scratch(halves, cols, cols),
            scratch(halves, cols, cols),
            scratch(halves, cols, cols),
            scratch(rows, cols),
            scratch(2, halves, 24, cols),
            scratch(2, halves, 16, cols),
            scratch(2, 21, 1, cols),
            scratch(2, 15, 1, cols),
            scratch(2, 12, 1, cols),
            scratch(2, halves, 16, cols),
            scratch(2, halves, 24, cols),
            scratch(2, 15, 1, cols),
            scratch(2, 21, 1, cols),
            scratch(nlon, 12, 1, cols),
            scratch(nlon, 12, 1, cols),
            scratch(12, 1, cols),
            pltpu.SemaphoreType.DMA((2, 4)),
            pltpu.SemaphoreType.DMA((2, 4)),
            pltpu.SemaphoreType.DMA((2, nlon - 1)),
            pltpu.SemaphoreType.DMA((2, nlon - 1)),
        ],
        compiler_params=pltpu.CompilerParams(
            collective_id=0, has_side_effects=True, vmem_limit_bytes=24 * 1024 * 1024
        ),
    )(fold_map, tracers, east_courant, north_courant, east_kappa, north_kappa, ocean_mask)


def solution(mesh):
    in_specs = (
        P(None, None, "lat", "lon"),
        P(None, "lat", "lon"),
        P(None, "lat", "lon"),
        P(None, "lat", "lon"),
        P(None, "lat", "lon"),
        P(None, "lat", "lon"),
        P("lon"),
    )
    out_specs = P(None, None, "lat", "lon")
    return jax.shard_map(local, mesh=mesh, in_specs=in_specs, out_specs=out_specs, check_vma=False)
```

time: 113 us -> 22.7 us (0.20)
  the two profiles are of different devices: /device:TPU:11 before, /device:TPU:7 now
where the time goes in v1:
time: 22.7 us; the launch traced here: 22.3 us
  Pallas kernels  14.6 us (64%)
  local copies, waits for them, and re-layouts  7.65 us (34%)
    pallas_call x1, Pallas kernels, local(): pl.pallas_call(functools.partial(kernel, nlat, nlon), out_shape=jax.Shape...  14.6 us
    unnamed x15, local copies, waits for them, and re-layouts  7.65 us

profile of v1, /device:TPU:7, one launch (start us, length us, event | category | flops | bytes accessed | tf_op | source)
XLA Modules:
  0.0 22.3 jit_solution(13058506335470559615)
XLA Ops:
  0.0 0.0 copy-start
  0.0 1.1 %copy-done = f32[2,3,256,128]{3,2,1,0:T(8,128)S(1)} copy-done((f32[2,3,256,128]{3,2,1,0:T(8,128)S(1)}, f32[2,3,256,128]{3,2,1,0:T(8,128)}, u32[]{:S(2)}) %copy-start) | copy-done | bytes 786456
  1.1 0.0 copy-start.1
  1.1 1.0 %copy-done.1 = f32[3,256,128]{2,1,0:T(8,128)S(1)} copy-done((f32[3,256,128]{2,1,0:T(8,128)S(1)}, f32[3,256,128]{2,1,0:T(8,128)}, u32[]{:S(2)}) %copy-start.1) | copy-done | bytes 393240
  2.1 0.0 copy-start.2
  2.1 1.0 %copy-done.2 = f32[3,256,128]{2,1,0:T(8,128)S(1)} copy-done((f32[3,256,128]{2,1,0:T(8,128)S(1)}, f32[3,256,128]{2,1,0:T(8,128)}, u32[]{:S(2)}) %copy-start.2) | copy-done | bytes 393240
  3.1 0.0 copy-start.3
  3.1 1.0 %copy-done.3 = f32[3,256,128]{2,1,0:T(8,128)S(1)} copy-done((f32[3,256,128]{2,1,0:T(8,128)S(1)}, f32[3,256,128]{2,1,0:T(8,128)}, u32[]{:S(2)}) %copy-start.3) | copy-done | bytes 393240
  4.1 0.0 copy-start.4
  4.1 1.0 %copy-done.4 = f32[3,256,128]{2,1,0:T(8,128)S(1)} copy-done((f32[3,256,128]{2,1,0:T(8,128)S(1)}, f32[3,256,128]{2,1,0:T(8,128)}, u32[]{:S(2)}) %copy-start.4) | copy-done | bytes 393240
  5.1 0.0 copy-start.5
  5.1 1.0 %copy-done.5 = s32[3,256,128]{2,1,0:T(8,128)S(1)} copy-done((s32[3,256,128]{2,1,0:T(8,128)S(1)}, s32[3,256,128]{2,1,0:T(8,128)}, u32[]{:S(2)}) %copy-start.5) | copy-done | bytes 393240
  6.1 0.0 copy-start.6
  6.1 0.7 %copy-done.6 = s32[128]{0:T(128)S(1)} copy-done((s32[128]{0:T(128)S(1)}, s32[128]{0:T(128)}, u32[]{:S(2)}) %copy-start.6) | copy-done | bytes 536
  6.8 14.6 %shard_map.73 = f32[2,3,256,128]{3,2,1,0:T(8,128)S(1)} custom-call(s32[128]{0:T(128)S(1)} %copy-done.6, f32[2,3,256,128]{3,2,1,0:T(8,128)S(1)} %copy-done, f32[3,256,128]{2,1,0:T(8,128)S(1)} %copy-done.1, f32[3,256,128]{2,1,0:T(8,128)S(1)} %copy-done.2, f32[3,256,128]{2,1,0:T(8,128)S(1)} %copy-done.3, f32[3,256,128]{2,1,0:T(8,128)S(1)} %copy-done.4, ...), custom_call_target="tpu_custom_call" | custom-call | tf_op jit(solution)/shard_map/pallas_call | solution.py:409
  21.4 0.9 %copy.9 = f32[2,3,256,128]{3,2,1,0:T(8,128)} copy(f32[2,3,256,128]{3,2,1,0:T(8,128)S(1)} %shard_map.73) | data formatting | bytes 1572864
Async XLA Ops:
  0.0 1.1 %copy-start = (f32[2,3,256,128]{3,2,1,0:T(8,128)S(1)}, f32[2,3,256,128]{3,2,1,0:T(8,128)}, u32[]{:S(2)}) copy-start(f32[2,3,256,128]{3,2,1,0:T(8,128)} %tr.1) | copy-start | bytes 2359300
  1.1 1.0 %copy-start.1 = (f32[3,256,128]{2,1,0:T(8,128)S(1)}, f32[3,256,128]{2,1,0:T(8,128)}, u32[]{:S(2)}) copy-start(f32[3,256,128]{2,1,0:T(8,128)} %ec.1) | copy-start | bytes 1179652
  2.1 1.0 %copy-start.2 = (f32[3,256,128]{2,1,0:T(8,128)S(1)}, f32[3,256,128]{2,1,0:T(8,128)}, u32[]{:S(2)}) copy-start(f32[3,256,128]{2,1,0:T(8,128)} %nc.1) | copy-start | bytes 1179652
  3.1 1.0 %copy-start.3 = (f32[3,256,128]{2,1,0:T(8,128)S(1)}, f32[3,256,128]{2,1,0:T(8,128)}, u32[]{:S(2)}) copy-start(f32[3,256,128]{2,1,0:T(8,128)} %ek.1) | copy-start | bytes 1179652
  4.1 1.0 %copy-start.4 = (f32[3,256,128]{2,1,0:T(8,128)S(1)}, f32[3,256,128]{2,1,0:T(8,128)}, u32[]{:S(2)}) copy-start(f32[3,256,128]{2,1,0:T(8,128)} %nk.1) | copy-start | bytes 1179652
  5.1 1.0 %copy-start.5 = (s32[3,256,128]{2,1,0:T(8,128)S(1)}, s32[3,256,128]{2,1,0:T(8,128)}, u32[]{:S(2)}) copy-start(s32[3,256,128]{2,1,0:T(8,128)} %mask.1) | copy-start | bytes 1179652
  6.1 0.7 %copy-start.6 = (s32[128]{0:T(128)S(1)}, s32[128]{0:T(128)}, u32[]{:S(2)}) copy-start(s32[128]{0:T(128)} %fold_ref.1) | copy-start | bytes 1540

commit v2 on v1

--- a/solution.py
+++ b/solution.py
@@ -10,7 +10,7 @@
 MESH = pl.DeviceIdType.MESH
 F32 = jnp.float32
 TOP = 16
-BLOCK = 64
+BLOCK = 32
 
 
 def face_flux(behind, center, forward, beyond, courant, diffusivity, opened):
@@ -45,12 +45,22 @@
 
 
 def kernel(
-    nlat, nlon, fold_ref, tr, ec, nc, ek, nk, mask, out,
+    nlat, nlon, fold_ref, tr_in, ec_in, nc_in, ek_in, nk_in, mask_in, result,
+    tr, ec, nc, ek, nk, mask, out, flow, load_sem, store_sem,
     s0, s1, ocean, we, wn, packed, t0, t1, ct, ce,
     se, sw, sn, ss, sf, re, rw, rn, rs, rf0, rf1, north_rows,
     send_sem, recv_sem, fold_send, fold_recv,
 ):
     levels, rows, cols = mask.shape
+    loads = {}
+    for i, (name, src, dst) in enumerate(
+        (
+            ("tr", tr_in, tr), ("mask", mask_in, mask), ("nc", nc_in, nc),
+            ("nk", nk_in, nk), ("ec", ec_in, ec), ("ek", ek_in, ek),
+        )
+    ):
+        loads[name] = pltpu.make_async_copy(src, dst, load_sem.at[i])
+        loads[name].start()
     lat = lax.axis_index("lat")
     lon = lax.axis_index("lon")
     southern = lat == 0
@@ -93,12 +103,15 @@
             for s in (s0, s1):
                 s[t * levels + l, 0:TOP, :] = jnp.zeros((TOP, cols), F32)
                 s[t * levels + l, TOP + rows : TOP + rows + 8, :] = jnp.zeros((8, cols), F32)
-        wn[0, l, 0:8, :] = jnp.zeros((8, cols), F32)
-        wn[1, l, 0:8, :] = jnp.zeros((8, cols), F32)
-        wn[2, l, 0:8, :] = jnp.zeros((8, cols), F32)
         return carry
 
+    loads["tr"].wait()
+    loads["mask"].wait()
     lax.fori_loop(0, levels, level_setup, 0)
+    for t in range(2):
+        flow[t, 0:8, :] = jnp.zeros((8, cols), F32)
+    loads["nc"].wait()
+    loads["nk"].wait()
 
     def row(s, r):
         return s[:, TOP + r : TOP + r + 1, :]
@@ -186,6 +199,9 @@
         pl.semaphore_wait(barrier, 4)
 
     start_lat(0)
+
+    loads["ec"].wait()
+    loads["ek"].wait()
 
     def pack(fields, target):
         for r in starts:
@@ -232,9 +248,9 @@
             u = nc[l, r : r + BLOCK, :]
             opened = o * ocean[l, r + 1 : r + 1 + BLOCK, :]
             ahead, center, forward, far = face_weights(u, nk[l, r : r + BLOCK, :], opened)
-            wn[0, l, 8 + r : 8 + r + BLOCK, :] = center
-            wn[1, l, 8 + r : 8 + r + BLOCK, :] = forward
-            wn[2, l, 8 + r : 8 + r + BLOCK, :] = far
+            wn[0, l, r : r + BLOCK, :] = center
+            wn[1, l, r : r + BLOCK, :] = forward
+            wn[2, l, r : r + BLOCK, :] = far
         return carry
 
     lax.fori_loop(0, levels, level_weights, 0)
@@ -245,9 +261,9 @@
                 ea = we[0, l, r : r + BLOCK, :]
                 eb = we[1, l, r : r + BLOCK, :]
                 ee = we[2, l, r : r + BLOCK, :]
-                na = wn[0, l, r : r + BLOCK + 8, :]
-                nb = wn[1, l, r : r + BLOCK + 8, :]
-                ne = wn[2, l, r : r + BLOCK + 8, :]
+                na = wn[0, l, r : r + BLOCK, :]
+                nb = wn[1, l, r : r + BLOCK, :]
+                ne = wn[2, l, r : r + BLOCK, :]
                 o = ocean[l, r : r + BLOCK, :]
                 for t in range(2):
                     f = t * levels + l
@@ -256,12 +272,12 @@
                     far = jnp.where(ee <= 0.0, pltpu.roll(q, 1, 1), pltpu.roll(q, cols - 2, 1))
                     flux = ea * q + eb * pltpu.roll(q, cols - 1, 1) + ee * far
                     total = q - flux + pltpu.roll(flux, 1, 1)
-                    b = s[f, base - 8 : base + BLOCK, :]
-                    a = s[f, base - 9 : base + BLOCK - 1, :]
-                    c = s[f, base - 7 : base + BLOCK + 1, :]
-                    d = s[f, base - 6 : base + BLOCK + 2, :]
-                    flux = na * b + nb * c + ne * jnp.where(ne <= 0.0, a, d)
-                    total = total - flux[8:] + flux[7 : 7 + BLOCK]
+                    a = s[f, base - 1 : base + BLOCK - 1, :]
+                    c = s[f, base + 1 : base + BLOCK + 1, :]
+                    d = s[f, base + 2 : base + BLOCK + 2, :]
+                    flux = na * q + nb * c + ne * jnp.where(ne <= 0.0, a, d)
+                    flow[t, 8 + r : 8 + r + BLOCK, :] = flux
+                    total = total - flux + flow[t, 7 + r : 7 + r + BLOCK, :]
                     put(t, l, r, o * total)
             return carry
 
@@ -338,14 +354,15 @@
                 ):
                     ct[h, pl.ds(4 * t * levels + j, levels, stride=4), :] = fix
 
-    def spread_columns(add):
+    def spread_columns(add, done):
         edge = (lane < 2) | (lane >= cols - 2)
         for h in halves:
             ce[h * cols : (h + 1) * cols, :] = ct[h].T
-        for r in starts:
-            x = ce[r : r + BLOCK, :]
-            for f in range(n):
+        for f in range(n):
+            for r in starts:
+                x = ce[r : r + BLOCK, :]
                 add(f, r, jnp.where(edge, pltpu.roll(x, (cols - 4 * f - 2) % cols, 1), 0.0))
+            done(f)
 
     advance(s0, put_s1)
     for h in halves:
@@ -374,7 +391,7 @@
         at = slice(TOP + r, TOP + r + BLOCK)
         s1[f, at, :] = s1[f, at, :] + value
 
-    spread_columns(add_s1)
+    spread_columns(add_s1, lambda f: None)
     fill_rows(1, s1)
     start_lat(1)
     advance(s1, put_out)
@@ -392,7 +409,13 @@
         t, l = divmod(f, levels)
         out[t, l, r : r + BLOCK, :] = out[t, l, r : r + BLOCK, :] + value
 
-    spread_columns(add_out)
+    def store(f):
+        t, l = divmod(f, levels)
+        return pltpu.make_async_copy(out.at[t, l], result.at[t, l], store_sem.at[f])
+
+    spread_columns(add_out, lambda f: store(f).start())
+    for f in range(n):
+        store(f).wait()
 
 
 def local(tracers, east_courant, north_courant, east_kappa, north_kappa, ocean_mask, fold_map):
@@ -405,18 +428,27 @@
     def scratch(*shape):
         return pltpu.VMEM(shape, F32)
 
-    whole = pl.BlockSpec(memory_space=pltpu.VMEM)
     return pl.pallas_call(
         functools.partial(kernel, nlat, nlon),
         out_shape=jax.ShapeDtypeStruct(tracers.shape, F32),
-        in_specs=[pl.BlockSpec(memory_space=pltpu.SMEM)] + [whole] * 6,
-        out_specs=whole,
+        in_specs=[pl.BlockSpec(memory_space=pltpu.SMEM)] + [pl.BlockSpec(memory_space=pltpu.HBM)] * 6,
+        out_specs=pl.BlockSpec(memory_space=pltpu.HBM),
         scratch_shapes=[
+            scratch(2, levels, rows, cols),
+            scratch(levels, rows, cols),
+            scratch(levels, rows, cols),
+            scratch(levels, rows, cols),
+            scratch(levels, rows, cols),
+            pltpu.VMEM((levels, rows, cols), jnp.int32),
+            scratch(2, levels, rows, cols),
+            scratch(2, rows + 8, cols),
+            pltpu.SemaphoreType.DMA((6,)),
+            pltpu.SemaphoreType.DMA((fields,)),
             scratch(fields, TOP + rows + 8, cols),
             scratch(fields, TOP + rows + 8, cols),
             scratch(levels, rows + 8, cols),
             scratch(3, levels, rows, cols),
-            scratch(3, levels, rows + 8, cols),
+            scratch(3, levels, rows, cols),
             scratch(rows, cols),
             scratch(halves, cols, cols),
             scratch(halves, cols, cols),
@@ -440,7 +472,7 @@
             pltpu.SemaphoreType.DMA((2, nlon - 1)),
         ],
         compiler_params=pltpu.CompilerParams(
-            collective_id=0, has_side_effects=True, vmem_limit_bytes=24 * 1024 * 1024
+            collective_id=0, has_side_effects=True, vmem_limit_bytes=58 * 1024 * 1024
         ),
     )(fold_map, tracers, east_courant, north_courant, east_kappa, north_kappa, ocean_mask)
 

time: 22.7 us -> 17.9 us (0.79)
  local copies, waits for them, and re-layouts: 7.65 us -> 2.06 us
  Pallas kernels: 14.6 us -> 15.6 us
    unnamed x15 -> x1, local copies, waits for them, and re-layouts: 7.65 us -> 2.06 us
    pallas_call x1, Pallas kernels: 14.6 us -> 15.6 us  [local(): pl.pallas_call(functools.partial(kernel, nlat, nlon), out_shape=jax.Shape...]
where the time goes in v2:
time: 17.9 us; the launch traced here: 17.7 us
  Pallas kernels  15.6 us (87%)
  local copies, waits for them, and re-layouts  2.06 us (12%)
    pallas_call x1, Pallas kernels, local(): pl.pallas_call(functools.partial(kernel, nlat, nlon), out_shape=jax.Shape...  15.6 us
    unnamed x1, local copies, waits for them, and re-layouts  2.06 us

profile of v2, /device:TPU:7, one launch (start us, length us, event | category | flops | bytes accessed | tf_op | source)
XLA Modules:
  0.0 17.7 jit_solution(10228642464157961956)
XLA Ops:
  0.0 15.6 %shard_map.73 = f32[2,3,256,128]{3,2,1,0:T(8,128)} custom-call(s32[128]{0:T(128)} %fold_ref.1, f32[2,3,256,128]{3,2,1,0:T(8,128)} %tr_in.1, f32[3,256,128]{2,1,0:T(8,128)} %ec_in.1, f32[3,256,128]{2,1,0:T(8,128)} %nc_in.1, f32[3,256,128]{2,1,0:T(8,128)} %ek_in.1, f32[3,256,128]{2,1,0:T(8,128)} %nk_in.1, s32[3,256,128]{2,1,0:T(8,128)} %mask_in.1), custom_call_target="tpu_custom_call" | custom-call | tf_op jit(solution)/shard_map/pallas_call | solution.py:431
  15.6 2.1 %copy.9 = f32[2,3,256,128]{3,2,1,0:T(8,128)} copy(f32[2,3,256,128]{3,2,1,0:T(8,128)} %shard_map.73) | data formatting | bytes 1572864

commit v3 on v2

--- a/solution.py
+++ b/solution.py
@@ -45,8 +45,8 @@
 
 
 def kernel(
-    nlat, nlon, fold_ref, tr_in, ec_in, nc_in, ek_in, nk_in, mask_in, result,
-    tr, ec, nc, ek, nk, mask, out, flow, load_sem, store_sem,
+    nlat, nlon, fold_ref, tr_in, ec_in, nc_in, ek_in, nk_in, mask_in, out,
+    tr, ec, nc, ek, nk, mask, flow, load_sem,
     s0, s1, ocean, we, wn, packed, t0, t1, ct, ce,
     se, sw, sn, ss, sf, re, rw, rn, rs, rf0, rf1, north_rows,
     send_sem, recv_sem, fold_send, fold_recv,
@@ -354,15 +354,16 @@
                 ):
                     ct[h, pl.ds(4 * t * levels + j, levels, stride=4), :] = fix
 
-    def spread_columns(add, done):
-        edge = (lane < 2) | (lane >= cols - 2)
+    def turn_columns():
         for h in halves:
             ce[h * cols : (h + 1) * cols, :] = ct[h].T
+
+    def spread_columns(add, blocks):
+        edge = (lane < 2) | (lane >= cols - 2)
         for f in range(n):
-            for r in starts:
+            for r in blocks:
                 x = ce[r : r + BLOCK, :]
                 add(f, r, jnp.where(edge, pltpu.roll(x, (cols - 4 * f - 2) % cols, 1), 0.0))
-            done(f)
 
     advance(s0, put_s1)
     for h in halves:
@@ -391,9 +392,11 @@
         at = slice(TOP + r, TOP + r + BLOCK)
         s1[f, at, :] = s1[f, at, :] + value
 
-    spread_columns(add_s1, lambda f: None)
+    turn_columns()
+    spread_columns(add_s1, (starts[0], starts[-1]))
     fill_rows(1, s1)
     start_lat(1)
+    spread_columns(add_s1, starts[1:-1])
     advance(s1, put_out)
     wait_lat(1)
     to_east(1).wait()
@@ -409,13 +412,8 @@
         t, l = divmod(f, levels)
         out[t, l, r : r + BLOCK, :] = out[t, l, r : r + BLOCK, :] + value
 
-    def store(f):
-        t, l = divmod(f, levels)
-        return pltpu.make_async_copy(out.at[t, l], result.at[t, l], store_sem.at[f])
-
-    spread_columns(add_out, lambda f: store(f).start())
-    for f in range(n):
-        store(f).wait()
+    turn_columns()
+    spread_columns(add_out, starts)
 
 
 def local(tracers, east_courant, north_courant, east_kappa, north_kappa, ocean_mask, fold_map):
@@ -430,9 +428,9 @@
 
     return pl.pallas_call(
         functools.partial(kernel, nlat, nlon),
-        out_shape=jax.ShapeDtypeStruct(tracers.shape, F32),
+        out_shape=pltpu.VMEM(tracers.shape, F32),
         in_specs=[pl.BlockSpec(memory_space=pltpu.SMEM)] + [pl.BlockSpec(memory_space=pltpu.HBM)] * 6,
-        out_specs=pl.BlockSpec(memory_space=pltpu.HBM),
+        out_specs=pl.BlockSpec(memory_space=pltpu.VMEM),
         scratch_shapes=[
             scratch(2, levels, rows, cols),
             scratch(levels, rows, cols),
@@ -440,10 +438,8 @@
             scratch(levels, rows, cols),
             scratch(levels, rows, cols),
             pltpu.VMEM((levels, rows, cols), jnp.int32),
-            scratch(2, levels, rows, cols),
             scratch(2, rows + 8, cols),
             pltpu.SemaphoreType.DMA((6,)),
-            pltpu.SemaphoreType.DMA((fields,)),
             scratch(fields, TOP + rows + 8, cols),
             scratch(fields, TOP + rows + 8, cols),
             scratch(levels, rows + 8, cols),
@@ -472,9 +468,15 @@
             pltpu.SemaphoreType.DMA((2, nlon - 1)),
         ],
         compiler_params=pltpu.CompilerParams(
-            collective_id=0, has_side_effects=True, vmem_limit_bytes=58 * 1024 * 1024
+            collective_id=0, has_side_effects=True, vmem_limit_bytes=55 * 1024 * 1024
         ),
-    )(fold_map, tracers, east_courant, north_courant, east_kappa, north_kappa, ocean_mask)
+    )(
+        fold_map,
+        *(
+            pltpu.with_memory_space_constraint(x, pltpu.HBM)
+            for x in (tracers, east_courant, north_courant, east_kappa, north_kappa, ocean_mask)
+        ),
+    )
 
 
 def solution(mesh):

time: 17.9 us -> 15.7 us (0.88)
  local copies, waits for them, and re-layouts: 2.06 us -> 0.88 us
  Pallas kernels: 15.6 us -> 14.7 us
    unnamed x1, local copies, waits for them, and re-layouts: 2.06 us -> 0.88 us
    pallas_call x1, Pallas kernels: 15.6 us -> 14.7 us  [local(): pl.pallas_call(functools.partial(kernel, nlat, nlon), out_shape=pltpu.VME...]
where the time goes in v3:
time: 15.7 us; the launch traced here: 15.6 us
  Pallas kernels  14.7 us (94%)
  local copies, waits for them, and re-layouts  0.88 us (6%)
    pallas_call x1, Pallas kernels, local(): pl.pallas_call(functools.partial(kernel, nlat, nlon), out_shape=pltpu.VME...  14.7 us
    unnamed x1, local copies, waits for them, and re-layouts  0.88 us

profile of v3, /device:TPU:7, one launch (start us, length us, event | category | flops | bytes accessed | tf_op | source)
XLA Modules:
  0.0 15.6 jit_solution(9238926693087736081)
XLA Ops:
  0.0 14.7 %shard_map.73 = f32[2,3,256,128]{3,2,1,0:T(8,128)S(1)} custom-call(s32[128]{0:T(128)} %fold_ref.1, f32[2,3,256,128]{3,2,1,0:T(8,128)} %tr_in.1, f32[3,256,128]{2,1,0:T(8,128)} %ec_in.1, f32[3,256,128]{2,1,0:T(8,128)} %nc_in.1, f32[3,256,128]{2,1,0:T(8,128)} %ek_in.1, f32[3,256,128]{2,1,0:T(8,128)} %nk_in.1, s32[3,256,128]{2,1,0:T(8,128)} %mask_in.1), custom_call_target="tpu_custom_call" | custom-call | tf_op jit(solution)/shard_map/pallas_call | solution.py:429
  14.7 0.9 %copy.9 = f32[2,3,256,128]{3,2,1,0:T(8,128)} copy(f32[2,3,256,128]{3,2,1,0:T(8,128)S(1)} %shard_map.73) | data formatting | bytes 1572864

commit v4 on v3

--- a/solution.py
+++ b/solution.py
@@ -10,7 +10,7 @@
 MESH = pl.DeviceIdType.MESH
 F32 = jnp.float32
 TOP = 16
-BLOCK = 32
+BLOCK = 16
 
 
 def face_flux(behind, center, forward, beyond, courant, diffusivity, opened):

time: 15.7 us -> 18.2 us (1.16)
  Pallas kernels: 14.7 us -> 17.2 us
    pallas_call x1, Pallas kernels: 14.7 us -> 17.2 us  [local(): pl.pallas_call(functools.partial(kernel, nlat, nlon), out_shape=pltpu.VME...]
where the time goes in v4:
time: 18.2 us; the launch traced here: 18.1 us
  Pallas kernels  17.2 us (95%)
  local copies, waits for them, and re-layouts  0.88 us (5%)
    pallas_call x1, Pallas kernels, local(): pl.pallas_call(functools.partial(kernel, nlat, nlon), out_shape=pltpu.VME...  17.2 us
    unnamed x1, local copies, waits for them, and re-layouts  0.88 us

profile of v4, /device:TPU:7, one launch (start us, length us, event | category | flops | bytes accessed | tf_op | source)
XLA Modules:
  0.0 18.1 jit_solution(16771216888787018034)
XLA Ops:
  0.0 17.2 %shard_map.73 = f32[2,3,256,128]{3,2,1,0:T(8,128)S(1)} custom-call(s32[128]{0:T(128)} %fold_ref.1, f32[2,3,256,128]{3,2,1,0:T(8,128)} %tr_in.1, f32[3,256,128]{2,1,0:T(8,128)} %ec_in.1, f32[3,256,128]{2,1,0:T(8,128)} %nc_in.1, f32[3,256,128]{2,1,0:T(8,128)} %ek_in.1, f32[3,256,128]{2,1,0:T(8,128)} %nk_in.1, s32[3,256,128]{2,1,0:T(8,128)} %mask_in.1), custom_call_target="tpu_custom_call" | custom-call | tf_op jit(solution)/shard_map/pallas_call | solution.py:429
  17.2 0.9 %copy.9 = f32[2,3,256,128]{3,2,1,0:T(8,128)} copy(f32[2,3,256,128]{3,2,1,0:T(8,128)S(1)} %shard_map.73) | data formatting | bytes 1572864
